TPU v7x, 32 devices: a whole 2x2x4 slice. The times are simulated.
32 devices in a mesh: req: 8 (over z, y), tp: 4 (over x, core).
Axes of the slice: x: 2, y: 2, z: 4, core: 2. Of those that a mesh axis runs over, the one named last changes fastest.
Arguments:
- queries: bfloat16 [8, 1280, 24, 128], P('req', None, 'tp'), may hold values from -25 to 25
- text_kv: bfloat16 [8, 1280, 4, 256], P('req', None, 'tp'), may hold values from -6 to 6
- image_rows: bfloat16 [4096, 6144], P('req', 'tp'), may hold values from -6 to 6
- row_request: int32 [4096], P('req'), may hold values from 0 to 7, as said below
- row_position: int32 [4096], P('req'), may hold values from 8 to 1263, as said below
- prompt_lengths: int32 [8], P('req'), may hold values from 24 to 1280, as said below
- kv_weight: bfloat16 [6144, 4, 256], P('tp'), may hold values from -0.078125 to 0.078125
Outputs:
- attended: bfloat16 [8, 1280, 24, 128], P('req', None, 'tp')
Inputs may be any that keep to these rules, and one draw needn't show every extreme that they name: `row_request`: the rows of one device name one request at most 128 times, and on every device some request is named exactly 128 times. `row_position`: the rows naming one request take distinct positions, 8 or more, that form one run ending at least 16 positions before that request's length. `prompt_lengths`: some request has length exactly 1280.
All inputs are finite; a program needn't handle non-finite values.
Results may differ from a plain program's by a relative error of at most 0.0085.
Values may be sent and summed in bfloat16 or wider, within the bound.
A program may use at most 128 MiB of HBM per device.

v0:
```python
import math

import jax
import jax.numpy as jnp
from jax import lax
from jax.sharding import PartitionSpec as P


def rotate_keys(summed, positions, head_dim):
    half = head_dim // 2
    freqs = jnp.exp(jnp.arange(half, dtype=jnp.float32) * (-2.0 * math.log(1000000.0) / head_dim))
    angles = positions.astype(jnp.float32)[:, None, None] * freqs[None, None, :]
    cosine = jnp.cos(angles)
    sine = jnp.sin(angles)
    first = summed[..., :half]
    second = summed[..., half:head_dim]
    rotated = jnp.concatenate(
        [first * cosine - second * sine, second * cosine + first * sine, summed[..., head_dim:]],
        axis=-1,
    )
    return rotated.astype(jnp.bfloat16)


def per_device(queries, text_kv, image_rows, row_request, row_position, prompt_lengths, kv_weight):
    groups = lax.axis_size("req")
    own_rows = image_rows.shape[0]
    capacity = 2 * own_rows // groups
    prompt = queries.shape[1]
    head_dim = queries.shape[3]
    local_heads = kv_weight.shape[1] // lax.axis_size("tp")
    one_hot = (row_request[:, None] == jnp.arange(groups, dtype=jnp.int32)[None, :]).astype(
        jnp.int32
    )
    before = jnp.cumsum(one_hot, axis=0) - one_hot
    slot_index = jnp.sum(before * one_hot, axis=1)
    target = row_request * capacity + slot_index
    pos_buffer = (
        jnp.full((groups * capacity,), prompt, jnp.int32)
        .at[target]
        .set(row_position)
        .reshape(groups, capacity)
    )
    row_buffer = (
        jnp.zeros((groups * capacity, image_rows.shape[1]), jnp.bfloat16).at[target].set(image_rows)
    )
    row_buffer = row_buffer.reshape(groups, capacity, image_rows.shape[1])
    got_rows, got_pos = (
        lax.all_to_all(row_buffer, "req", split_axis=0, concat_axis=0, tiled=True),
        lax.all_to_all(pos_buffer, "req", split_axis=0, concat_axis=0, tiled=True),
    )
    flat_rows = got_rows.reshape(groups * capacity, image_rows.shape[1])
    places = got_pos.reshape(groups * capacity)
    summed = lax.psum_scatter(
        jnp.einsum("rd,dhc->hrc", flat_rows, kv_weight, preferred_element_type=jnp.float32),
        "tp",
        scatter_dimension=0,
        tiled=True,
    )
    image_kv = rotate_keys(jnp.transpose(summed, (1, 0, 2)), places, head_dim)
    prompt_kv = text_kv[0].at[places].set(image_kv, mode="drop")
    length = prompt_lengths[0]
    local_query_heads = queries.shape[2]
    group = local_query_heads // local_heads
    grouped = queries[0].reshape(prompt, local_heads, group, head_dim)
    keys = prompt_kv[..., :head_dim]
    values = prompt_kv[..., head_dim:]
    block = prompt // 2
    pieces = []
    for block_index in range(2):
        row_start = block_index * block
        query_block = grouped[row_start : row_start + block]
        scores = jnp.einsum(
            "qhgd,khd->hgqk", query_block, keys, preferred_element_type=jnp.float32
        ) * head_dim ** (-0.5)
        query_index = row_start + jnp.arange(block, dtype=jnp.int32)
        key_index = jnp.arange(prompt, dtype=jnp.int32)
        allowed = (key_index[None, :] <= query_index[:, None]) & (key_index[None, :] < length)
        scores = jnp.where(allowed, scores, jnp.float32(-1e30))
        highest = jnp.max(scores, axis=-1, keepdims=True)
        expo = jnp.exp(scores - highest)
        weights = (expo / jnp.sum(expo, axis=-1, keepdims=True)).astype(jnp.bfloat16)
        result = jnp.einsum("hgqk,khd->qhgd", weights, values, preferred_element_type=jnp.float32)
        result = jnp.where(query_index[:, None, None, None] < length, result, jnp.float32(0.0))
        pieces.append(result.reshape(block, local_query_heads, head_dim).astype(jnp.bfloat16))
    return jnp.concatenate(pieces, axis=0)[None]


def solution(mesh):
    in_specs = (
        P("req", None, "tp", None),
        P("req", None, "tp", None),
        P("req", "tp"),
        P("req"),
        P("req"),
        P("req"),
        P("tp", None, None),
    )
    out_specs = P("req", None, "tp", None)
    return jax.shard_map(
        per_device, mesh=mesh, in_specs=in_specs, out_specs=out_specs, check_vma=False
    )
```

profile of v0, /device:TPU:0, one launch (start us, length us, event | category | flops | bytes accessed | tf_op | source)
XLA Modules:
  0.0 221.2 jit_solution(8242725893636036156)
XLA Ops:
  6.5 0.0 copy-start
  6.5 0.0 reduce-scatter.2.cloned.1.call-start
  6.5 0.8 fusion.41
  7.4 1.1 reduce-window.6
  8.5 0.2 slice_reduce_fusion
  8.8 0.8 fusion.40
  9.5 0.7 compare_select_fusion.1
  10.2 6.0 %scatter_custom_fusion.1 = bf16[1024,1536]{1,0:T(8,128)(2,1)} fusion(s32[512]{0:T(512)S(1)} %compare_select_fusion.1, bf16[512,1536]{1,0:T(8,128)(2,1)} %param.9, bf16[]{:T(256)} %constant.4.clone.1), kind=kCustom, calls=%fused_computation.27 | custom fusion | bytes 3146240 | tf_op jit(solution)/shard_map/scatter | solution.py:44
  16.2 78.0 %all_to_all.14 = bf16[8,128,1536]{2,1,0:T(8,128)(2,1)S(1)} all-to-all(bf16[8,128,1536]{2,1,0:T(8,128)(2,1)} %bitcast.107), channel_id=1, replica_groups=mesh['req'=8,'tp'=4] {'req'}, dimensions={0} | all-to-all | bytes 6291456 | tf_op jit(solution)/shard_map/all_to_all | solution.py:48
  94.2 0.0 copy-done
  94.2 5.0 %fusion.10 = f32[4,1024,256]{1,2,0:T(8,128)} fusion(bf16[1024,1536,1]{1,0,2:T(8,128)(2,1)S(1)} %bitcast.108, bf16[1536,4,256]{2,1,0:T(4,128)(2,1)S(1)} %copy-done), kind=kOutput, calls=%fused_computation.21 | convolution fusion | flops 3221225472 | bytes 10485760 | tf_op jit(solution)/shard_map/rd,dhc->hrc/dot_general | solution.py:54
  99.2 0.0 copy-start.3
  99.2 0.0 reduce-scatter.2.cloned.1.call-update
  99.2 3.3 %scatter_custom_fusion = s32[1024]{0:T(1024)} fusion(s32[512]{0:T(512)S(1)} %compare_select_fusion.1, s32[512]{0:T(512)} %param.11, s32[]{:T(128)} %constant.11.clone.1), kind=kCustom, calls=%fused_computation.61 | custom fusion | bytes 4608 | tf_op jit(solution)/shard_map/scatter | solution.py:40
  102.5 3.6 %all-to-all-start = ((s32[8,1,128]{2,1,0:T(1,128)}), s32[8,1,128]{2,1,0:T(1,128)S(1)}, u32[]{:S(2)}, u32[]{:S(2)}) async-start(s32[8,1,128]{2,1,0:T(1,128)} %bitcast.5), calls=%async_computation | async-start | bytes 8192 | tf_op jit(solution)/shard_map/all_to_all | solution.py:49
  106.8 1.6 fusion.6
  108.5 4.0 %all-to-all-done = s32[8,1,128]{2,1,0:T(1,128)S(1)} async-done(((s32[8,1,128]{2,1,0:T(1,128)}), s32[8,1,128]{2,1,0:T(1,128)S(1)}, u32[]{:S(2)}, u32[]{:S(2)}) %all-to-all-start) | async-done | bytes 4128 | tf_op jit(solution)/shard_map/all_to_all | solution.py:49
  112.5 30.4 %reduce-scatter.2.cloned.1.call-done = f32[1,1024,256]{1,2,0:T(8,128)} async-done(((f32[4,1024,256]{1,2,0:T(8,128)}), f32[1,1024,256]{1,2,0:T(8,128)}) %reduce-scatter.2.cloned.1.call-update) | async-done | bytes 1048592 | tf_op jit(solution)/shard_map/reduce_scatter | solution.py:53
  142.9 1.1 slice.65
  143.9 2.1 fusion.36
  146.1 0.8 maximum_bitcast_fusion.1
  146.9 1.2 copy.29
  148.2 0.0 copy-done.3
  148.2 5.5 %scatter_fusion = bf16[1280,256]{1,0:T(8,128)(2,1)S(1)} fusion(bf16[1280,256]{1,0:T(8,128)(2,1)S(1)} %bitcast.106, s32[1024]{0:T(1024)S(1)} %bitcast.112, bf16[1024,256]{1,0:T(8,128)(2,1)S(1)} %copy.29), kind=kCustom, calls=%fused_computation.2 | custom fusion | bytes 1576960 | tf_op jit(solution)/shard_map/scatter | solution.py:60
  153.6 0.0 copy-start.2
  153.6 0.0 copy-start.4
  153.6 10.0 %fusion.44 = (f32[6,640]{1,0:T(8,128)S(1)}, f32[1,6,640,1280]{2,3,1,0:T(8,128)}) fusion(bf16[1,1280,6,128]{3,1,2,0:T(8,128)(2,1)} %param.7, bf16[1280,1,256]{2,0,1:T(8,128)(2,1)S(1)} %bitcast.102, pred[640,1280]{0,1:T(8,128)(4,1)S(1)} %get-tuple-element.8), kind=kOutput, calls=%fused_computation.65 | convolution fusion | flops 1273032960 | bytes 21806080 | tf_op jit(solution)/shard_map/qhgd,khd->hgqk/dot_general | solution.py:72
  163.6 0.0 copy-done.4
  163.6 8.5 %fusion.45 = (f32[6,640]{1,0:T(8,128)S(1)}, f32[1,6,640,1280]{2,3,1,0:T(8,128)}) fusion(bf16[1,1280,6,128]{3,1,2,0:T(8,128)(2,1)S(1)} %copy-done.4, bf16[1280,1,256]{2,0,1:T(8,128)(2,1)S(1)} %bitcast.103, pred[640,1280]{0,1:T(8,128)(4,1)S(1)} %get-tuple-element.7), kind=kOutput, calls=%fused_computation.66 | convolution fusion | flops 1273032960 | bytes 21806080 | tf_op jit(solution)/shard_map/qhgd,khd->hgqk/dot_general | solution.py:72
  172.1 9.2 %fusion.1 = f32[6,640]{1,0:T(8,128)S(1)} fusion(f32[1,6,640,1280]{2,3,1,0:T(8,128)} %get-tuple-element.10, f32[6,640]{1,0:T(8,128)S(1)} %get-tuple-element.9), kind=kLoop, calls=%fused_computation.10 | loop fusion | flops 9826560 | bytes 19691520 | tf_op jit(solution)/shard_map/reduce_sum | solution.py:81
  181.2 0.0 copy-done.2
  181.3 9.7 %fusion.24 = bf16[640,6,128]{0,2,1:T(8,128)(2,1)} fusion(f32[6,640]{1,0:T(8,128)S(1)} %fusion.1, f32[1,6,640,1280]{2,3,1,0:T(8,128)} %get-tuple-element.10, f32[6,640]{1,0:T(8,128)S(1)} %get-tuple-element.9, pred[640]{0:T(1024)(128)(4,1)S(1)} %get-tuple-element.14, bf16[1280,1,256]{2,0,1:T(8,128)(2,1)S(1)} %bitcast.104), kind=kOutput, calls=%fused_computation.30 | convolution fusion | flops 1274019840 | bytes 21013504 | tf_op jit(solution)/shard_map/hgqk,khd->qhgd/dot_general | solution.py:82
  190.9 9.2 %fusion = f32[6,640]{1,0:T(8,128)S(1)} fusion(f32[1,6,640,1280]{2,3,1,0:T(8,128)} %get-tuple-element.12, f32[6,640]{1,0:T(8,128)S(1)} %get-tuple-element.11), kind=kLoop, calls=%fused_computation.9 | loop fusion | flops 9826560 | bytes 19691520 | tf_op jit(solution)/shard_map/reduce_sum | solution.py:81
  200.1 0.0 copy-start.5
  200.1 0.0 copy-start.1
  200.1 8.9 %fusion.21 = bf16[640,6,128]{0,2,1:T(8,128)(2,1)S(1)} fusion(f32[6,640]{1,0:T(8,128)S(1)} %fusion, f32[1,6,640,1280]{2,3,1,0:T(8,128)} %get-tuple-element.12, f32[6,640]{1,0:T(8,128)S(1)} %get-tuple-element.11, pred[640]{0:T(1024)(128)(4,1)S(1)} %get-tuple-element.13, bf16[1280,1,256]{2,0,1:T(8,128)(2,1)} %bitcast.105), kind=kOutput, calls=%fused_computation.29 | convolution fusion | flops 1274019840 | bytes 21002880 | tf_op jit(solution)/shard_map/hgqk,khd->qhgd/dot_general | solution.py:82
  208.9 0.0 copy-done.5
  209.0 1.4 maximum_bitcast_fusion
  210.4 3.9 %copy.34 = bf16[1,1280,6,128]{3,1,2,0:T(8,128)(2,1)} copy(bf16[1,1280,6,128]{1,3,2,0:T(8,128)(2,1)} %maximum_bitcast_fusion) | data formatting | bytes 3932160 | tf_op jit(solution)/shard_map/broadcast_in_dim | solution.py:85
  214.3 0.0 copy-done.1
  (8 shorter events, 0.1 us)
Async XLA Ops:
  6.5 87.6 %copy-start = (bf16[1536,4,256]{2,1,0:T(4,128)(2,1)S(1)}, bf16[1536,4,256]{2,1,0:T(4,128)(2,1)}, u32[]{:S(2)}) copy-start(bf16[1536,4,256]{2,1,0:T(4,128)(2,1)} %param.13) | copy-start | bytes 9437188
  6.5 136.3 %reduce-scatter.2.cloned.1.call-start = ((), (), s32[]{:S(2)}) async-start(), calls=%async_computation.3 | async-start | bytes 5242880 | tf_op jit(solution)/shard_map/reduce_scatter | solution.py:53
  99.2 49.0 %copy-start.3 = (bf16[1,1280,1,256]{3,1,2,0:T(8,128)(2,1)S(1)}, bf16[1,1280,1,256]{3,1,2,0:T(8,128)(2,1)}, u32[]{:S(2)}) copy-start(bf16[1,1280,1,256]{3,1,2,0:T(8,128)(2,1)} %param.8) | copy-start | bytes 1966084
  102.5 10.0 %all-to-all-start = ((s32[8,1,128]{2,1,0:T(1,128)}), s32[8,1,128]{2,1,0:T(1,128)S(1)}, u32[]{:S(2)}, u32[]{:S(2)}) async-start(s32[8,1,128]{2,1,0:T(1,128)} %bitcast.5), calls=%async_computation | async-start | bytes 8192 | tf_op jit(solution)/shard_map/all_to_all | solution.py:49
  153.6 27.6 %copy-start.2 = (bf16[1280,256]{1,0:T(8,128)(2,1)}, bf16[1280,256]{1,0:T(8,128)(2,1)S(1)}, u32[]{:S(2)}) copy-start(bf16[1280,256]{1,0:T(8,128)(2,1)S(1)} %scatter_fusion) | copy-start | bytes 1966084
  153.6 10.0 %copy-start.4 = (bf16[1,1280,6,128]{3,1,2,0:T(8,128)(2,1)S(1)}, bf16[1,1280,6,128]{3,1,2,0:T(8,128)(2,1)}, u32[]{:S(2)}) copy-start(bf16[1,1280,6,128]{3,1,2,0:T(8,128)(2,1)} %param.7) | copy-start | bytes 5898244
  200.1 8.9 %copy-start.5 = (bf16[640,6,128]{0,2,1:T(8,128)(2,1)S(1)}, bf16[640,6,128]{0,2,1:T(8,128)(2,1)}, u32[]{:S(2)}) copy-start(bf16[640,6,128]{0,2,1:T(8,128)(2,1)} %fusion.24) | copy-start | bytes 2949124
  200.1 14.3 %copy-start.1 = (bf16[1536,4,256]{2,1,0:T(4,128)(2,1)S(1)}, bf16[1536,4,256]{2,1,0:T(4,128)(2,1)}, u32[]{:S(2)}) copy-start(bf16[1536,4,256]{2,1,0:T(4,128)(2,1)} %param.13) | copy-start | bytes 9437188
Sparse Core Ops, SparseCore 0:
  99.3 43.4 reduce-scatter.1
where the time goes:
time: 222 us; the launch traced here: 221 us
  blocking collectives  78 us (35%)
  matrix products  42 us (19%)
  waiting for transfers between devices  34.4 us (15%)
  other arithmetic  27.8 us (13%)
  local copies, waits for them, and re-layouts  21.2 us (10%)
  between operations  14.2 us (6%)
  starting transfers between devices  3.59 us (2%)
    all_to_all x1, blocking collectives, per_device(): lax.all_to_all(row_buffer, 'req', split_axis=0, concat_axis=0, tiled=True)  78 us
    reduce_scatter x1, waiting for transfers between devices, per_device(): lax.psum_scatter(jnp.einsum('rd,dhc->hrc', flat_rows, kv_weight, preferre...  30.4 us
    dot_general x2, matrix products, per_device(): jnp.einsum('hgqk,khd->qhgd', weights, values, preferred_element_type=jnp....  18.5 us
    dot_general x2, matrix products, per_device(): jnp.einsum('qhgd,khd->hgqk', query_block, keys, preferred_element_type=jn...  18.4 us
    reduce_sum x2, other arithmetic, per_device(): jnp.sum(expo, axis=-1, keepdims=True)  18.3 us
    scatter x1, local copies, waits for them, and re-layouts, per_device(): jnp.zeros((groups * capacity, image_rows.shape[1]), jnp.bfloat16).at[target]  5.96 us
    scatter x1, local copies, waits for them, and re-layouts, per_device(): prompt_kv = text_kv[0].at[places].set(image_kv, mode='drop')  5.46 us
    dot_general x1, matrix products, per_device(): jnp.einsum('rd,dhc->hrc', flat_rows, kv_weight, preferred_element_type=jn...  5.01 us
  transfers between devices with their start and end apart: 2, of which 2 were waited for; matrix products, arithmetic and copies ran while one was open for 2% of the time, Pallas kernels for 0%

commit v1 on v0

v1 whole, which is shorter than its diff:
```python
import functools
import math

import jax
import jax.numpy as jnp
import numpy as np
from jax import lax
from jax.experimental import pallas as pl
from jax.experimental.pallas import tpu as pltpu
from jax.sharding import PartitionSpec as P

MESH = pl.DeviceIdType.MESH
NT = (((1,), (1,)), ((), ()))
VMEM = pltpu.VMEM
Q_BLOCK = 256


def route_kernel(
    groups,
    capacity,
    partial_ref,
    request_ref,
    position_ref,
    freq_ref,
    kv_ref,
    place_ref,
    from_core,
    to_chip,
    from_chip,
    hot_ref,
    bins_ref,
    place_bins,
    core_send,
    core_recv,
    chip_send,
    chip_recv,
    kv_send,
    kv_recv,
    place_send,
    place_recv,
):
    me = lax.axis_index("req")
    tp = lax.axis_index("tp")
    side = lax.rem(tp, 2)
    half = tp // 2
    mate = half * 2 + (1 - side)
    far = (1 - half) * 2 + side
    rows = partial_ref.shape[1]
    width = kv_ref.shape[2]

    barrier = pltpu.get_barrier_semaphore()

    def greet(step, carry):
        pl.semaphore_signal(
            barrier, inc=1, device_id={"req": lax.rem(me + step, groups)}, device_id_type=MESH
        )
        return carry

    lax.fori_loop(1, groups, greet, 0)
    for partner in (mate, far):
        pl.semaphore_signal(barrier, inc=1, device_id={"tp": partner}, device_id_type=MESH)

    request = request_ref[...]
    hot = (request == lax.broadcasted_iota(jnp.int32, (groups, rows), 0)).astype(jnp.float32)
    row_id = lax.broadcasted_iota(jnp.int32, (rows, rows), 0)
    column_id = lax.broadcasted_iota(jnp.int32, (rows, rows), 1)
    earlier = (row_id < column_id).astype(jnp.float32).astype(jnp.bfloat16)
    before = jnp.dot(hot.astype(jnp.bfloat16), earlier, preferred_element_type=jnp.float32)
    rank = jnp.sum(before * hot, axis=0, keepdims=True)
    target = request.astype(jnp.float32) * float(capacity) + rank
    position = position_ref[...]

    pl.semaphore_wait(barrier, groups + 1)

    def core_copy(part):
        columns = pl.ds(part * width, width)
        copies = []
        for index in range(2):
            copies.append(
                pltpu.make_async_remote_copy(
                    src_ref=partial_ref.at[index * 2 + 1 - side, :, columns],
                    dst_ref=from_core.at[part, index],
                    send_sem=core_send.at[part, index],
                    recv_sem=core_recv.at[part, index],
                    device_id={"tp": mate},
                    device_id_type=MESH,
                )
            )
        return copies

    core_copies = [core_copy(part) for part in range(2)]
    for part in range(2):
        for index in range(2):
            core_copies[part][index].start()

    slots = groups * capacity
    hot_ref[...] = (
        (target == lax.broadcasted_iota(jnp.int32, (slots, rows), 0).astype(jnp.float32))
        .astype(jnp.float32)
        .astype(jnp.bfloat16)
    )
    coded = position + 1
    line = lax.broadcasted_iota(jnp.int32, (16, rows), 0)
    digits = (
        jnp.where(line < 8, coded // 32, lax.rem(coded, 32)).astype(jnp.float32).astype(jnp.bfloat16)
    )

    def place_copy(dest):
        return pltpu.make_async_remote_copy(
            src_ref=place_bins.at[dest],
            dst_ref=place_ref.at[me],
            send_sem=place_send.at[dest],
            recv_sem=place_recv.at[me],
            device_id={"req": dest},
            device_id_type=MESH,
        )

    def bin_places(dest):
        found = lax.dot_general(
            digits,
            hot_ref[pl.ds(pl.multiple_of(dest * capacity, capacity), capacity), :],
            NT,
            preferred_element_type=jnp.float32,
        )
        return (found[:8] * 32.0 + found[8:]).astype(jnp.int32)

    def send_places(step, carry):
        dest = lax.rem(me + step, groups)
        place_bins[dest] = bin_places(dest)
        place_copy(dest).start()
        return carry

    lax.fori_loop(1, groups, send_places, 0)
    place_ref[me] = bin_places(me)

    chip_copies = []
    for part in range(2):
        columns = pl.ds(part * width, width)
        for index in range(2):
            core_copies[part][index].wait()
        other = 1 - half
        to_chip[part] = (
            partial_ref[other * 2 + side, :, columns] + from_core[part, other]
        ).astype(jnp.bfloat16)
        copy = pltpu.make_async_remote_copy(
            src_ref=to_chip.at[part],
            dst_ref=from_chip.at[part],
            send_sem=chip_send.at[part],
            recv_sem=chip_recv.at[part],
            device_id={"tp": far},
            device_id_type=MESH,
        )
        copy.start()
        chip_copies.append(copy)

    place_column = jnp.sum(
        jnp.where(row_id == column_id, position.astype(jnp.float32), 0.0), axis=1, keepdims=True
    )
    angle = place_column * freq_ref[...]
    cosine = jnp.cos(angle)
    lane = lax.broadcasted_iota(jnp.int32, (rows, width), 1)
    sine = jnp.where(lane < width // 2, -1.0, 1.0) * jnp.sin(angle)

    def kv_copy(part, dest):
        return pltpu.make_async_remote_copy(
            src_ref=bins_ref.at[part, dest],
            dst_ref=kv_ref.at[part, pl.ds(pl.multiple_of(me * capacity, capacity), capacity)],
            send_sem=kv_send.at[part, dest],
            recv_sem=kv_recv.at[part, me],
            device_id={"req": dest},
            device_id_type=MESH,
        )

    for part in range(2):
        columns = pl.ds(part * width, width)
        chip_copies[part].wait()
        summed = (
            partial_ref[half * 2 + side, :, columns]
            + from_core[part, half]
            + from_chip[part].astype(jnp.float32)
        )
        if part == 0:
            summed = summed * cosine + pltpu.roll(summed, width // 2, 1) * sine
        image = summed.astype(jnp.bfloat16)

        def bin_rows(dest, image=image):
            return jnp.dot(
                hot_ref[pl.ds(pl.multiple_of(dest * capacity, capacity), capacity), :],
                image,
                preferred_element_type=jnp.float32,
            ).astype(jnp.bfloat16)

        def send_rows(step, carry, part=part, bin_rows=bin_rows):
            dest = lax.rem(me + step, groups)
            bins_ref[part, dest] = bin_rows(dest)
            kv_copy(part, dest).start()
            return carry

        lax.fori_loop(1, groups, send_rows, 0)
        kv_ref[part, pl.ds(pl.multiple_of(me * capacity, capacity), capacity)] = bin_rows(me)

    def finish(step, carry):
        peer = lax.rem(me + step, groups)
        place_copy(peer).wait_send()
        pltpu.make_async_copy(
            place_bins.at[peer], place_ref.at[peer], place_recv.at[peer]
        ).wait()
        for part in range(2):
            kv_copy(part, peer).wait_send()
            pltpu.make_async_copy(
                bins_ref.at[part, peer],
                kv_ref.at[part, pl.ds(pl.multiple_of(peer * capacity, capacity), capacity)],
                kv_recv.at[part, peer],
            ).wait()
        return carry

    lax.fori_loop(1, groups, finish, 0)


def route(partial, row_request, row_position, groups, capacity):
    heads, rows, both = partial.shape
    width = both // 2
    slots = groups * capacity
    exponent = np.arange(width // 2, dtype=np.float32) * np.float32(
        -2.0 * math.log(1000000.0) / width
    )
    freqs = np.exp(exponent.astype(np.float32)).astype(np.float32)
    freqs = jnp.asarray(np.concatenate([freqs, freqs])[None])
    vmem = pl.BlockSpec(memory_space=VMEM)
    return pl.pallas_call(
        functools.partial(route_kernel, groups, capacity),
        out_shape=(
            jax.ShapeDtypeStruct((2, slots, width), jnp.bfloat16),
            jax.ShapeDtypeStruct((groups, 8, capacity), jnp.int32),
        ),
        in_specs=[vmem] * 4,
        out_specs=(vmem, vmem),
        scratch_shapes=[
            VMEM((2, 2, rows, width), jnp.float32),
            VMEM((2, rows, width), jnp.bfloat16),
            VMEM((2, rows, width), jnp.bfloat16),
            VMEM((slots, rows), jnp.bfloat16),
            VMEM((2, groups, capacity, width), jnp.bfloat16),
            VMEM((groups, 8, capacity), jnp.int32),
            pltpu.SemaphoreType.DMA((2, 2)),
            pltpu.SemaphoreType.DMA((2, 2)),
            pltpu.SemaphoreType.DMA((2,)),
            pltpu.SemaphoreType.DMA((2,)),
            pltpu.SemaphoreType.DMA((2, groups)),
            pltpu.SemaphoreType.DMA((2, groups)),
            pltpu.SemaphoreType.DMA((groups,)),
            pltpu.SemaphoreType.DMA((groups,)),
        ],
        compiler_params=pltpu.CompilerParams(
            collective_id=0, has_side_effects=True, vmem_limit_bytes=32 * 1024 * 1024
        ),
        name="route",
    )(partial, row_request[None], row_position[None], freqs)


def attend_kernel(length_ref, query_ref, text_ref, kv_ref, place_ref, out_ref, keys, values):
    prompt, width = keys.shape
    slots = kv_ref.shape[1]

    @pl.when(pl.program_id(0) == 0)
    def _():
        if place_ref.shape[0] > 1:
            places = jnp.concatenate(
                [place_ref[source, 0:1, :] for source in range(place_ref.shape[0])], axis=1
            )
        else:
            places = place_ref[0, 0:1, :]
        places = places - 1
        first = jnp.min(jnp.where(places < 0, prompt, places), axis=1, keepdims=True)
        last = jnp.max(places, axis=1, keepdims=True)
        for start in range(0, prompt, Q_BLOCK):
            block = pl.ds(start, Q_BLOCK)
            index = lax.broadcasted_iota(jnp.int32, (Q_BLOCK, slots), 0) + start
            hot = (index == places).astype(jnp.float32).astype(jnp.bfloat16)
            own = lax.broadcasted_iota(jnp.int32, (Q_BLOCK, width), 0) + start
            image = (own >= first) & (own <= last)
            for part, held in ((0, keys), (1, values)):
                found = jnp.dot(hot, kv_ref[part], preferred_element_type=jnp.float32)
                text = text_ref[block, part * width : (part + 1) * width].astype(jnp.float32)
                held[block, 0:width] = jnp.where(image, found, text).astype(jnp.bfloat16)
        values[:, width:] = jnp.ones((prompt, width), jnp.bfloat16)

    length = length_ref[0]
    factor = width**-0.5 * math.log2(math.e)
    for start in range(0, prompt, Q_BLOCK):
        stop = start + Q_BLOCK
        query = query_ref[0, start:stop, :]
        scores = lax.dot_general(query, keys[:stop], NT, preferred_element_type=jnp.float32)
        row = lax.broadcasted_iota(jnp.int32, (Q_BLOCK, Q_BLOCK), 0)
        column = lax.broadcasted_iota(jnp.int32, (Q_BLOCK, Q_BLOCK), 1)
        diagonal = jnp.where(column <= row, scores[:, start:], jnp.float32(-1e30))
        if start:
            scores = jnp.concatenate([scores[:, :start], diagonal], axis=1)
        else:
            scores = diagonal
        highest = jnp.max(scores, axis=1, keepdims=True)
        expo = jnp.exp2((scores - highest) * factor).astype(jnp.bfloat16)
        result = jnp.dot(expo, values[:stop], preferred_element_type=jnp.float32)
        own = lax.broadcasted_iota(jnp.int32, (Q_BLOCK, width), 0) + start
        attended = jnp.where(own < length, result[:, :width] / result[:, width:], 0.0)
        out_ref[0, start:stop, :] = attended.astype(jnp.bfloat16)


def attend(queries, text, kv, places, lengths):
    heads, prompt, width = queries.shape
    return pl.pallas_call(
        attend_kernel,
        out_shape=jax.ShapeDtypeStruct(queries.shape, jnp.bfloat16),
        grid_spec=pltpu.PrefetchScalarGridSpec(
            num_scalar_prefetch=1,
            grid=(heads,),
            in_specs=[
                pl.BlockSpec((1, prompt, width), lambda head, _: (head, 0, 0)),
                pl.BlockSpec(text.shape, lambda head, _: (0, 0)),
                pl.BlockSpec(kv.shape, lambda head, _: (0, 0, 0)),
                pl.BlockSpec(places.shape, lambda head, _: (0, 0, 0)),
            ],
            out_specs=pl.BlockSpec((1, prompt, width), lambda head, _: (head, 0, 0)),
            scratch_shapes=[
                VMEM((prompt, width), jnp.bfloat16),
                VMEM((prompt, 2 * width), jnp.bfloat16),
            ],
        ),
        compiler_params=pltpu.CompilerParams(vmem_limit_bytes=48 * 1024 * 1024),
        name="attend",
    )(lengths, queries, text, kv, places)


def per_device(queries, text_kv, image_rows, row_request, row_position, prompt_lengths, kv_weight):
    groups = lax.axis_size("req")
    capacity = 2 * image_rows.shape[0] // groups
    partial = jnp.einsum(
        "rd,dhc->hrc", image_rows, kv_weight, preferred_element_type=jnp.float32
    )
    kv, places = route(partial, row_request, row_position, groups, capacity)
    if capacity % 128:
        places = jnp.broadcast_to(places[:, 0, :].reshape(1, 1, -1), (1, 8, groups * capacity))
    attended = attend(
        jnp.transpose(queries[0], (1, 0, 2)), text_kv[0, :, 0, :], kv, places, prompt_lengths
    )
    return jnp.transpose(attended, (1, 0, 2))[None]


def solution(mesh):
    in_specs = (
        P("req", None, "tp", None),
        P("req", None, "tp", None),
        P("req", "tp"),
        P("req"),
        P("req"),
        P("req"),
        P("tp", None, None),
    )
    out_specs = P("req", None, "tp", None)
    return jax.shard_map(
        per_device, mesh=mesh, in_specs=in_specs, out_specs=out_specs, check_vma=False
    )
```

time: 222 us -> 47.4 us (0.21)
  blocking collectives: 78 us -> 0 us
  Pallas kernels: 0 us -> 41.4 us
  matrix products: 42 us -> 3.26 us
  waiting for transfers between devices: 34.4 us -> 0 us
  other arithmetic: 27.8 us -> 0 us
  local copies, waits for them, and re-layouts: 21.2 us -> 1.9 us
  between operations: 14.2 us -> 0.71 us
  starting transfers between devices: 3.59 us -> 0 us
    all_to_all x1 -> x0, blocking collectives: 78 us -> none  [per_device(): lax.all_to_all(row_buffer, 'req', split_axis=0, concat_axis=0, tiled=True)]
    pallas_call x0 -> x2, Pallas kernels: none -> 41.4 us  [the longest x1 24.7 us: route(): pl.pallas_call(functools.partial(route_kernel, groups, capacity), out_sha...]
    dot_general x5 -> x1, matrix products: 42 us -> 3.26 us  [per_device(): jnp.einsum('rd,dhc->hrc', image_rows, kv_weight, preferred_element_type=j...]
    reduce_scatter x1 -> x0, waiting for transfers between devices: 30.4 us -> none  [per_device(): lax.psum_scatter(jnp.einsum('rd,dhc->hrc', flat_rows, kv_weight, preferre...]
    reduce_sum x3 -> x0, other arithmetic: 19.1 us -> none  [the longest x2 18.3 us: per_device(): jnp.sum(expo, axis=-1, keepdims=True)]
    scatter x3 -> x0, local copies, waits for them, and re-layouts: 14.7 us -> none  [the longest x1 5.96 us: per_device(): jnp.zeros((groups * capacity, image_rows.shape[1]), jnp.bfloat16).at[target]]
    all_to_all x1 -> x0, waiting for transfers between devices: 4.03 us -> none  [per_device(): lax.all_to_all(pos_buffer, 'req', split_axis=0, concat_axis=0, tiled=True)]
    broadcast_in_dim x1 -> x0, local copies, waits for them, and re-layouts: 3.94 us -> none  [per_device(): return jnp.concatenate(pieces, axis=0)[None]]
  transfers between devices with their start and end apart: 2 -> 0, of which waited for: 2 -> 0; matrix products, arithmetic and copies ran while one was open for 2% -> 0% of each run, Pallas kernels for 0% -> 0%
where the time goes in v1:
time: 47.4 us; the launch traced here: 47.3 us
  Pallas kernels  41.4 us (87%)
  matrix products  3.26 us (7%)
  local copies, waits for them, and re-layouts  1.9 us (4%)
  between operations  0.71 us (1%)
    pallas_call x1, Pallas kernels, route(): pl.pallas_call(functools.partial(route_kernel, groups, capacity), out_sha...  24.7 us
    pallas_call x1, Pallas kernels, attend(): pl.pallas_call(attend_kernel, out_shape=jax.ShapeDtypeStruct(queries.shap...  16.7 us
    dot_general x1, matrix products, per_device(): jnp.einsum('rd,dhc->hrc', image_rows, kv_weight, preferred_element_type=j...  3.26 us
    unnamed x12, local copies, waits for them, and re-layouts  1.9 us

profile of v1, /device:TPU:0, one launch (start us, length us, event | category | flops | bytes accessed | tf_op | source)
XLA Modules:
  0.0 47.3 jit_solution(9198388487791577219)
XLA Ops:
  0.0 0.0 copy-start
  0.0 0.0 copy-start.5
  0.0 0.0 copy-start.3
  0.0 0.0 copy-start.4
  0.0 1.9 %copy-done = bf16[1536,4,256]{2,1,0:T(4,128)(2,1)S(1)} copy-done((bf16[1536,4,256]{2,1,0:T(4,128)(2,1)S(1)}, bf16[1536,4,256]{2,1,0:T(4,128)(2,1)}, u32[]{:S(2)}) %copy-start) | copy-done | bytes 3145752
  1.9 0.0 copy-start.2
  1.9 3.3 %fusion.2.partial_ref = f32[4,512,256]{2,1,0:T(8,128)S(1)} fusion(bf16[1536,4,256]{2,1,0:T(4,128)(2,1)S(1)} %copy-done, bf16[512,1536]{1,0:T(8,128)(2,1)} %param.10), kind=kOutput, calls=%fused_computation.2 | convolution fusion | flops 1610612736 | bytes 6815744 | tf_op jit(solution)/shard_map/rd,dhc->hrc/dot_general | solution.py:337
  5.2 0.0 copy-start.1
  5.2 0.0 copy-done.5
  5.2 0.0 copy-done.3
  5.2 0.0 copy-done.4
  5.2 24.7 %route.1 = (bf16[2,1024,128]{2,1,0:T(8,128)(2,1)S(1)}, s32[8,8,128]{2,1,0:T(8,128)S(1)}) custom-call(f32[4,512,256]{2,1,0:T(8,128)S(1)} %fusion.2.partial_ref, s32[1,512]{1,0:T(1,128)S(1)} %bitcast.16, s32[1,512]{1,0:T(1,128)S(1)} %bitcast.17, f32[1,128]{1,0:T(1,128)S(1)} %copy-done.5), custom_call_target="tpu_custom_call" | custom-call | tf_op jit(solution)/shard_map/route/pallas_call | solution.py:230
  30.5 0.0 copy-done.2
  30.5 0.0 copy-done.1
  30.6 16.7 %attend.1 = bf16[6,1280,128]{2,1,0:T(8,128)(2,1)} custom-call(s32[1]{0:T(128)S(6)} %copy.16.length_ref, bf16[6,1280,128]{2,1,0:T(8,128)(2,1)S(1)} %bitcast.14, bf16[1280,256]{1,0:T(8,128)(2,1)S(1)} %bitcast.15, bf16[2,1024,128]{2,1,0:T(8,128)(2,1)S(1)} %get-tuple-element.7.kv_ref, s32[8,8,128]{2,1,0:T(8,128)S(1)} %get-tuple-element.8.place_ref), custom_call_target="tpu_custom_call" | custom-call | tf_op jit(solution)/shard_map/attend/pallas_call | solution.py:311
Async XLA Ops:
  0.0 1.9 %copy-start = (bf16[1536,4,256]{2,1,0:T(4,128)(2,1)S(1)}, bf16[1536,4,256]{2,1,0:T(4,128)(2,1)}, u32[]{:S(2)}) copy-start(bf16[1536,4,256]{2,1,0:T(4,128)(2,1)} %param.14) | copy-start | bytes 9437188
  0.0 5.2 %copy-start.5 = (f32[1,128]{1,0:T(1,128)S(1)}, f32[1,128]{1,0:T(1,128)}, u32[]{:S(2)}) copy-start(f32[1,128]{1,0:T(1,128)} %constant.2.clone.freq_ref) | copy-start | bytes 1540
  0.0 5.2 %copy-start.3 = (s32[512]{0:T(512)S(1)}, s32[512]{0:T(512)}, u32[]{:S(2)}) copy-start(s32[512]{0:T(512)} %param.11) | copy-start | bytes 6148
  0.0 5.2 %copy-start.4 = (s32[512]{0:T(512)S(1)}, s32[512]{0:T(512)}, u32[]{:S(2)}) copy-start(s32[512]{0:T(512)} %param.12) | copy-start | bytes 6148
  1.9 28.6 %copy-start.2 = (bf16[1,1280,1,256]{3,1,2,0:T(8,128)(2,1)S(1)}, bf16[1,1280,1,256]{3,1,2,0:T(8,128)(2,1)}, u32[]{:S(2)}) copy-start(bf16[1,1280,1,256]{3,1,2,0:T(8,128)(2,1)} %param.9) | copy-start | bytes 1966084
  5.2 25.4 %copy-start.1 = (bf16[1,1280,6,128]{3,1,2,0:T(8,128)(2,1)S(1)}, bf16[1,1280,6,128]{3,1,2,0:T(8,128)(2,1)}, u32[]{:S(2)}) copy-start(bf16[1,1280,6,128]{3,1,2,0:T(8,128)(2,1)} %param.8) | copy-start | bytes 5898244

commit v2 on v1

--- a/solution.py
+++ b/solution.py
@@ -13,6 +13,7 @@
 NT = (((1,), (1,)), ((), ()))
 VMEM = pltpu.VMEM
 Q_BLOCK = 256
+HEAD_BLOCK = 3
 
 
 def route_kernel(
@@ -24,6 +25,7 @@
     freq_ref,
     kv_ref,
     place_ref,
+    to_core,
     from_core,
     to_chip,
     from_chip,
@@ -69,6 +71,8 @@
     rank = jnp.sum(before * hot, axis=0, keepdims=True)
     target = request.astype(jnp.float32) * float(capacity) + rank
     position = position_ref[...]
+    for index in range(2):
+        to_core[index] = partial_ref[index * 2 + 1 - side].astype(jnp.bfloat16)
 
     pl.semaphore_wait(barrier, groups + 1)
 
@@ -78,7 +82,7 @@
         for index in range(2):
             copies.append(
                 pltpu.make_async_remote_copy(
-                    src_ref=partial_ref.at[index * 2 + 1 - side, :, columns],
+                    src_ref=to_core.at[index, :, columns],
                     dst_ref=from_core.at[part, index],
                     send_sem=core_send.at[part, index],
                     recv_sem=core_recv.at[part, index],
@@ -140,7 +144,7 @@
             core_copies[part][index].wait()
         other = 1 - half
         to_chip[part] = (
-            partial_ref[other * 2 + side, :, columns] + from_core[part, other]
+            partial_ref[other * 2 + side, :, columns] + from_core[part, other].astype(jnp.float32)
         ).astype(jnp.bfloat16)
         copy = pltpu.make_async_remote_copy(
             src_ref=to_chip.at[part],
@@ -176,7 +180,7 @@
         chip_copies[part].wait()
         summed = (
             partial_ref[half * 2 + side, :, columns]
-            + from_core[part, half]
+            + from_core[part, half].astype(jnp.float32)
             + from_chip[part].astype(jnp.float32)
         )
         if part == 0:
@@ -236,7 +240,8 @@
         in_specs=[vmem] * 4,
         out_specs=(vmem, vmem),
         scratch_shapes=[
-            VMEM((2, 2, rows, width), jnp.float32),
+            VMEM((2, rows, both), jnp.bfloat16),
+            VMEM((2, 2, rows, width), jnp.bfloat16),
             VMEM((2, rows, width), jnp.bfloat16),
             VMEM((2, rows, width), jnp.bfloat16),
             VMEM((slots, rows), jnp.bfloat16),
@@ -287,23 +292,44 @@
 
     length = length_ref[0]
     factor = width**-0.5 * math.log2(math.e)
-    for start in range(0, prompt, Q_BLOCK):
-        stop = start + Q_BLOCK
-        query = query_ref[0, start:stop, :]
-        scores = lax.dot_general(query, keys[:stop], NT, preferred_element_type=jnp.float32)
-        row = lax.broadcasted_iota(jnp.int32, (Q_BLOCK, Q_BLOCK), 0)
-        column = lax.broadcasted_iota(jnp.int32, (Q_BLOCK, Q_BLOCK), 1)
-        diagonal = jnp.where(column <= row, scores[:, start:], jnp.float32(-1e30))
-        if start:
-            scores = jnp.concatenate([scores[:, :start], diagonal], axis=1)
-        else:
-            scores = diagonal
-        highest = jnp.max(scores, axis=1, keepdims=True)
-        expo = jnp.exp2((scores - highest) * factor).astype(jnp.bfloat16)
-        result = jnp.dot(expo, values[:stop], preferred_element_type=jnp.float32)
+    row = lax.broadcasted_iota(jnp.int32, (Q_BLOCK, Q_BLOCK), 0)
+    column = lax.broadcasted_iota(jnp.int32, (Q_BLOCK, Q_BLOCK), 1)
+
+    def score(head, start):
+        query = query_ref[head, start : start + Q_BLOCK, :]
+        blocks = []
+        for first in range(0, start + Q_BLOCK, Q_BLOCK):
+            block = lax.dot_general(
+                query, keys[first : first + Q_BLOCK], NT, preferred_element_type=jnp.float32
+            )
+            if first == start:
+                block = jnp.where(column <= row, block, jnp.float32(-1e30))
+            blocks.append(block)
+        return blocks
+
+    def weigh(head, start, blocks):
+        highest = jnp.max(functools.reduce(jnp.maximum, blocks), axis=1, keepdims=True)
+        result = None
+        for index, block in enumerate(blocks):
+            expo = jnp.exp2((block - highest) * factor).astype(jnp.bfloat16)
+            part = jnp.dot(
+                expo,
+                values[index * Q_BLOCK : (index + 1) * Q_BLOCK],
+                preferred_element_type=jnp.float32,
+            )
+            result = part if result is None else result + part
         own = lax.broadcasted_iota(jnp.int32, (Q_BLOCK, width), 0) + start
         attended = jnp.where(own < length, result[:, :width] / result[:, width:], 0.0)
-        out_ref[0, start:stop, :] = attended.astype(jnp.bfloat16)
+        out_ref[head, start : start + Q_BLOCK, :] = attended.astype(jnp.bfloat16)
+
+    steps = [
+        (head, start) for head in range(query_ref.shape[0]) for start in range(0, prompt, Q_BLOCK)
+    ]
+    held = score(*steps[0])
+    for index, step in enumerate(steps):
+        later = score(*steps[index + 1]) if index + 1 < len(steps) else None
+        weigh(*step, held)
+        held = later
 
 
 def attend(queries, text, kv, places, lengths):
@@ -313,14 +339,14 @@
         out_shape=jax.ShapeDtypeStruct(queries.shape, jnp.bfloat16),
         grid_spec=pltpu.PrefetchScalarGridSpec(
             num_scalar_prefetch=1,
-            grid=(heads,),
+            grid=(heads // HEAD_BLOCK,),
             in_specs=[
-                pl.BlockSpec((1, prompt, width), lambda head, _: (head, 0, 0)),
+                pl.BlockSpec((HEAD_BLOCK, prompt, width), lambda head, _: (head, 0, 0)),
                 pl.BlockSpec(text.shape, lambda head, _: (0, 0)),
                 pl.BlockSpec(kv.shape, lambda head, _: (0, 0, 0)),
                 pl.BlockSpec(places.shape, lambda head, _: (0, 0, 0)),
             ],
-            out_specs=pl.BlockSpec((1, prompt, width), lambda head, _: (head, 0, 0)),
+            out_specs=pl.BlockSpec((HEAD_BLOCK, prompt, width), lambda head, _: (head, 0, 0)),
             scratch_shapes=[
                 VMEM((prompt, width), jnp.bfloat16),
                 VMEM((prompt, 2 * width), jnp.bfloat16),

time: 47.4 us -> 41 us (0.86)
  Pallas kernels: 41.4 us -> 35 us
    pallas_call x1, Pallas kernels: 16.7 us -> 10.5 us  [attend(): pl.pallas_call(attend_kernel, out_shape=jax.ShapeDtypeStruct(queries.shap...]
where the time goes in v2:
time: 41 us; the launch traced here: 40.8 us
  Pallas kernels  35 us (85%)
  matrix products  3.26 us (8%)
  local copies, waits for them, and re-layouts  1.9 us (5%)
  between operations  0.71 us (2%)
    pallas_call x1, Pallas kernels, route(): pl.pallas_call(functools.partial(route_kernel, groups, capacity), out_sha...  24.5 us
    pallas_call x1, Pallas kernels, attend(): pl.pallas_call(attend_kernel, out_shape=jax.ShapeDtypeStruct(queries.shap...  10.5 us
    dot_general x1, matrix products, per_device(): jnp.einsum('rd,dhc->hrc', image_rows, kv_weight, preferred_element_type=j...  3.26 us
    unnamed x12, local copies, waits for them, and re-layouts  1.9 us

profile of v2, /device:TPU:0, one launch (start us, length us, event | category | flops | bytes accessed | tf_op | source)
XLA Modules:
  0.0 40.8 jit_solution(1812904744542057408)
XLA Ops:
  0.0 0.0 copy-start
  0.0 0.0 copy-start.5
  0.0 0.0 copy-start.3
  0.0 0.0 copy-start.4
  0.0 1.9 %copy-done = bf16[1536,4,256]{2,1,0:T(4,128)(2,1)S(1)} copy-done((bf16[1536,4,256]{2,1,0:T(4,128)(2,1)S(1)}, bf16[1536,4,256]{2,1,0:T(4,128)(2,1)}, u32[]{:S(2)}) %copy-start) | copy-done | bytes 3145752
  1.9 0.0 copy-start.2
  1.9 3.3 %fusion.2.partial_ref = f32[4,512,256]{2,1,0:T(8,128)S(1)} fusion(bf16[1536,4,256]{2,1,0:T(4,128)(2,1)S(1)} %copy-done, bf16[512,1536]{1,0:T(8,128)(2,1)} %param.10), kind=kOutput, calls=%fused_computation.2 | convolution fusion | flops 1610612736 | bytes 6815744 | tf_op jit(solution)/shard_map/rd,dhc->hrc/dot_general | solution.py:363
  5.2 0.0 copy-start.1
  5.2 0.0 copy-done.5
  5.2 0.0 copy-done.3
  5.2 0.0 copy-done.4
  5.2 24.5 %route.1 = (bf16[2,1024,128]{2,1,0:T(8,128)(2,1)S(1)}, s32[8,8,128]{2,1,0:T(8,128)S(1)}) custom-call(f32[4,512,256]{2,1,0:T(8,128)S(1)} %fusion.2.partial_ref, s32[1,512]{1,0:T(1,128)S(1)} %bitcast.16, s32[1,512]{1,0:T(1,128)S(1)} %bitcast.17, f32[1,128]{1,0:T(1,128)S(1)} %copy-done.5), custom_call_target="tpu_custom_call" | custom-call | tf_op jit(solution)/shard_map/route/pallas_call | solution.py:234
  30.3 0.0 copy-done.2
  30.4 0.0 copy-done.1
  30.4 10.5 %attend.1 = bf16[6,1280,128]{2,1,0:T(8,128)(2,1)} custom-call(s32[1]{0:T(128)S(6)} %copy.16.length_ref, bf16[6,1280,128]{2,1,0:T(8,128)(2,1)S(1)} %bitcast.14, bf16[1280,256]{1,0:T(8,128)(2,1)S(1)} %bitcast.15, bf16[2,1024,128]{2,1,0:T(8,128)(2,1)S(1)} %get-tuple-element.7.kv_ref, s32[8,8,128]{2,1,0:T(8,128)S(1)} %get-tuple-element.8.place_ref), custom_call_target="tpu_custom_call" | custom-call | tf_op jit(solution)/shard_map/attend/pallas_call | solution.py:337
Async XLA Ops:
  0.0 1.9 %copy-start = (bf16[1536,4,256]{2,1,0:T(4,128)(2,1)S(1)}, bf16[1536,4,256]{2,1,0:T(4,128)(2,1)}, u32[]{:S(2)}) copy-start(bf16[1536,4,256]{2,1,0:T(4,128)(2,1)} %param.14) | copy-start | bytes 9437188
  0.0 5.2 %copy-start.5 = (f32[1,128]{1,0:T(1,128)S(1)}, f32[1,128]{1,0:T(1,128)}, u32[]{:S(2)}) copy-start(f32[1,128]{1,0:T(1,128)} %constant.2.clone.freq_ref) | copy-start | bytes 1540
  0.0 5.2 %copy-start.3 = (s32[512]{0:T(512)S(1)}, s32[512]{0:T(512)}, u32[]{:S(2)}) copy-start(s32[512]{0:T(512)} %param.11) | copy-start | bytes 6148
  0.0 5.2 %copy-start.4 = (s32[512]{0:T(512)S(1)}, s32[512]{0:T(512)}, u32[]{:S(2)}) copy-start(s32[512]{0:T(512)} %param.12) | copy-start | bytes 6148
  1.9 28.5 %copy-start.2 = (bf16[1,1280,1,256]{3,1,2,0:T(8,128)(2,1)S(1)}, bf16[1,1280,1,256]{3,1,2,0:T(8,128)(2,1)}, u32[]{:S(2)}) copy-start(bf16[1,1280,1,256]{3,1,2,0:T(8,128)(2,1)} %param.9) | copy-start | bytes 1966084
  5.2 25.2 %copy-start.1 = (bf16[1,1280,6,128]{3,1,2,0:T(8,128)(2,1)S(1)}, bf16[1,1280,6,128]{3,1,2,0:T(8,128)(2,1)}, u32[]{:S(2)}) copy-start(bf16[1,1280,6,128]{3,1,2,0:T(8,128)(2,1)} %param.8) | copy-start | bytes 5898244

commit v3 on v2

--- a/solution.py
+++ b/solution.py
@@ -93,7 +93,7 @@
         return copies
 
     core_copies = [core_copy(part) for part in range(2)]
-    for part in range(2):
+    for part in (1, 0):
         for index in range(2):
             core_copies[part][index].start()
 
@@ -137,8 +137,8 @@
     lax.fori_loop(1, groups, send_places, 0)
     place_ref[me] = bin_places(me)
 
-    chip_copies = []
-    for part in range(2):
+    chip_copies = {}
+    for part in (1, 0):
         columns = pl.ds(part * width, width)
         for index in range(2):
             core_copies[part][index].wait()
@@ -155,15 +155,7 @@
             device_id_type=MESH,
         )
         copy.start()
-        chip_copies.append(copy)
-
-    place_column = jnp.sum(
-        jnp.where(row_id == column_id, position.astype(jnp.float32), 0.0), axis=1, keepdims=True
-    )
-    angle = place_column * freq_ref[...]
-    cosine = jnp.cos(angle)
-    lane = lax.broadcasted_iota(jnp.int32, (rows, width), 1)
-    sine = jnp.where(lane < width // 2, -1.0, 1.0) * jnp.sin(angle)
+        chip_copies[part] = copy
 
     def kv_copy(part, dest):
         return pltpu.make_async_remote_copy(
@@ -175,8 +167,16 @@
             device_id_type=MESH,
         )
 
-    for part in range(2):
+    for part in (1, 0):
         columns = pl.ds(part * width, width)
+        if part == 0:
+            place_column = jnp.sum(
+                jnp.where(row_id == column_id, position.astype(jnp.float32), 0.0), axis=1, keepdims=True
+            )
+            angle = place_column * freq_ref[...]
+            cosine = jnp.cos(angle)
+            lane = lax.broadcasted_iota(jnp.int32, (rows, width), 1)
+            sine = jnp.where(lane < width // 2, -1.0, 1.0) * jnp.sin(angle)
         chip_copies[part].wait()
         summed = (
             partial_ref[half * 2 + side, :, columns]

time: 41 us -> 40.9 us (level)
  no operation moved by 1% of the time
where the time goes in v3:
time: 40.9 us; the launch traced here: 40.7 us
  Pallas kernels  34.9 us (85%)
  matrix products  3.26 us (8%)
  local copies, waits for them, and re-layouts  1.9 us (5%)
  between operations  0.71 us (2%)
    pallas_call x1, Pallas kernels, route(): pl.pallas_call(functools.partial(route_kernel, groups, capacity), out_sha...  24.4 us
    pallas_call x1, Pallas kernels, attend(): pl.pallas_call(attend_kernel, out_shape=jax.ShapeDtypeStruct(queries.shap...  10.5 us
    dot_general x1, matrix products, per_device(): jnp.einsum('rd,dhc->hrc', image_rows, kv_weight, preferred_element_type=j...  3.26 us
    unnamed x12, local copies, waits for them, and re-layouts  1.9 us

profile of v3, /device:TPU:0, one launch (start us, length us, event | category | flops | bytes accessed | tf_op | source)
XLA Modules:
  0.0 40.7 jit_solution(13271345779481033807)
XLA Ops:
  0.0 0.0 copy-start
  0.0 0.0 copy-start.5
  0.0 0.0 copy-start.3
  0.0 0.0 copy-start.4
  0.0 1.9 %copy-done = bf16[1536,4,256]{2,1,0:T(4,128)(2,1)S(1)} copy-done((bf16[1536,4,256]{2,1,0:T(4,128)(2,1)S(1)}, bf16[1536,4,256]{2,1,0:T(4,128)(2,1)}, u32[]{:S(2)}) %copy-start) | copy-done | bytes 3145752
  1.9 0.0 copy-start.2
  1.9 3.3 %fusion.2.partial_ref = f32[4,512,256]{2,1,0:T(8,128)S(1)} fusion(bf16[1536,4,256]{2,1,0:T(4,128)(2,1)S(1)} %copy-done, bf16[512,1536]{1,0:T(8,128)(2,1)} %param.10), kind=kOutput, calls=%fused_computation.2 | convolution fusion | flops 1610612736 | bytes 6815744 | tf_op jit(solution)/shard_map/rd,dhc->hrc/dot_general | solution.py:363
  5.2 0.0 copy-start.1
  5.2 0.0 copy-done.5
  5.2 0.0 copy-done.3
  5.2 0.0 copy-done.4
  5.2 24.4 %route.1 = (bf16[2,1024,128]{2,1,0:T(8,128)(2,1)S(1)}, s32[8,8,128]{2,1,0:T(8,128)S(1)}) custom-call(f32[4,512,256]{2,1,0:T(8,128)S(1)} %fusion.2.partial_ref, s32[1,512]{1,0:T(1,128)S(1)} %bitcast.16, s32[1,512]{1,0:T(1,128)S(1)} %bitcast.17, f32[1,128]{1,0:T(1,128)S(1)} %copy-done.5), custom_call_target="tpu_custom_call" | custom-call | tf_op jit(solution)/shard_map/route/pallas_call | solution.py:234
  30.3 0.0 copy-done.2
  30.3 0.0 copy-done.1
  30.3 10.5 %attend.1 = bf16[6,1280,128]{2,1,0:T(8,128)(2,1)} custom-call(s32[1]{0:T(128)S(6)} %copy.16.length_ref, bf16[6,1280,128]{2,1,0:T(8,128)(2,1)S(1)} %bitcast.14, bf16[1280,256]{1,0:T(8,128)(2,1)S(1)} %bitcast.15, bf16[2,1024,128]{2,1,0:T(8,128)(2,1)S(1)} %get-tuple-element.7.kv_ref, s32[8,8,128]{2,1,0:T(8,128)S(1)} %get-tuple-element.8.place_ref), custom_call_target="tpu_custom_call" | custom-call | tf_op jit(solution)/shard_map/attend/pallas_call | solution.py:337
Async XLA Ops:
  0.0 1.9 %copy-start = (bf16[1536,4,256]{2,1,0:T(4,128)(2,1)S(1)}, bf16[1536,4,256]{2,1,0:T(4,128)(2,1)}, u32[]{:S(2)}) copy-start(bf16[1536,4,256]{2,1,0:T(4,128)(2,1)} %param.14) | copy-start | bytes 9437188
  0.0 5.2 %copy-start.5 = (f32[1,128]{1,0:T(1,128)S(1)}, f32[1,128]{1,0:T(1,128)}, u32[]{:S(2)}) copy-start(f32[1,128]{1,0:T(1,128)} %constant.2.clone.freq_ref) | copy-start | bytes 1540
  0.0 5.2 %copy-start.3 = (s32[512]{0:T(512)S(1)}, s32[512]{0:T(512)}, u32[]{:S(2)}) copy-start(s32[512]{0:T(512)} %param.11) | copy-start | bytes 6148
  0.0 5.2 %copy-start.4 = (s32[512]{0:T(512)S(1)}, s32[512]{0:T(512)}, u32[]{:S(2)}) copy-start(s32[512]{0:T(512)} %param.12) | copy-start | bytes 6148
  1.9 28.4 %copy-start.2 = (bf16[1,1280,1,256]{3,1,2,0:T(8,128)(2,1)S(1)}, bf16[1,1280,1,256]{3,1,2,0:T(8,128)(2,1)}, u32[]{:S(2)}) copy-start(bf16[1,1280,1,256]{3,1,2,0:T(8,128)(2,1)} %param.9) | copy-start | bytes 1966084
  5.2 25.1 %copy-start.1 = (bf16[1,1280,6,128]{3,1,2,0:T(8,128)(2,1)S(1)}, bf16[1,1280,6,128]{3,1,2,0:T(8,128)(2,1)}, u32[]{:S(2)}) copy-start(bf16[1,1280,6,128]{3,1,2,0:T(8,128)(2,1)} %param.8) | copy-start | bytes 5898244
